TPU v7x, 512 devices: a whole 4x8x8 slice. The times are simulated.
512 devices in a mesh: tok: 64 (over y, x, core), feat: 8 (over z).
Axes of the slice: x: 4, y: 8, z: 8, core: 2. Of those that a mesh axis runs over, the one named last changes fastest.
Arguments:
- activations: bfloat16 [131072, 8192], P('tok', 'feat'), may hold values from -200 to 200
- sketch: bfloat16 [8192, 256], P('feat'), may hold values from -0.0625 to 0.0625
Outputs:
- factor: float32 [256, 256], replicated
- projected: float32 [256, 8192], P('tok', 'feat')
All inputs are finite; a program needn't handle non-finite values.
Results may differ from a plain program's by a relative error of at most 0.014.
Values may be sent and summed in bfloat16 or wider, within the bound.
No kernel may reach another device: no remote copies, remote signals or barrier semaphores. Data moves between devices by JAX's collectives and lax.ppermute only.
A program may use at most 64 MiB of HBM per device.

v0:
```python
import math

import jax
import jax.numpy as jnp
from jax import lax
from jax.sharding import PartitionSpec as P


def inner_products(sketch_rows):
    return jnp.dot(
        sketch_rows.T,
        sketch_rows,
        precision=lax.Precision.HIGHEST,
        preferred_element_type=jnp.float32,
    )


def shards(activations, sketch):
    all_tokens = activations.shape[0] * lax.axis_size("tok")
    partial_value = jnp.dot(activations, sketch, preferred_element_type=jnp.float32)
    sketch_rows = lax.psum(partial_value.astype(jnp.bfloat16), "feat").astype(jnp.float32)
    gram_matrix = inner_products(sketch_rows)
    gram_matrix = lax.psum(gram_matrix, "tok") / all_tokens
    lower_factor = jnp.linalg.cholesky(gram_matrix)
    local_basis = lax.linalg.triangular_solve(
        lower_factor, sketch_rows.T, left_side=True, lower=True
    ).astype(jnp.bfloat16)
    own_rows = local_basis.shape[0] // lax.axis_size("tok")
    full_proj = jnp.dot(local_basis, activations, preferred_element_type=jnp.float32)
    summed = lax.psum(full_proj, "tok")
    projected = lax.dynamic_slice_in_dim(summed, lax.axis_index("tok") * own_rows, own_rows, 0)
    return (lower_factor.T, projected / math.sqrt(all_tokens))


def solution(mesh):
    in_specs = (P("tok", "feat"), P("feat", None))
    out_specs = (P(), P("tok", "feat"))
    return jax.shard_map(shards, mesh=mesh, in_specs=in_specs, out_specs=out_specs, check_vma=False)
```

profile of v0, /device:TPU:1, one launch (start us, length us, event | category | flops | bytes accessed | tf_op | source)
XLA Modules:
  0.0 557.2 jit_solution(7984248425359304730)
XLA Ops:
  7.2 0.0 all-reduce.5.cloned.1.call-start
  7.2 1.0 copy-done
  8.2 4.5 convolution_convert_fusion
  12.7 0.0 all-reduce.7.cloned.1.call-start
  12.8 84.0 %all-reduce.5.cloned.1.call-done = bf16[2048,256]{1,0:T(8,128)(2,1)} async-done(((bf16[2048,256]{1,0:T(8,128)(2,1)}), bf16[2048,256]{1,0:T(8,128)(2,1)}) %all-reduce.5.cloned.1.call-update) | async-done | bytes 1048592 | tf_op jit(solution)/shard_map/psum | solution.py:21
  96.8 2.9 fusion.16
  99.6 0.0 all-reduce.7.cloned.1.call-update
  99.6 0.0 all-reduce.9.cloned.1.call-start
  99.7 189.3 %all-reduce.7.cloned.1.call-done = f32[256,256]{0,1:T(8,128)} async-done(((f32[256,256]{0,1:T(8,128)}), f32[256,256]{0,1:T(8,128)}) %all-reduce.7.cloned.1.call-update) | async-done | bytes 262160 | tf_op jit(solution)/shard_map/psum | solution.py:23
  289.0 1.0 broadcast_multiply_fusion
  290.0 0.1 copy.5
  290.1 1.0 fusion.6
  291.2 11.7 %cholesky.50 = f32[128,128]{1,0:T(8,128)S(1)} custom-call(f32[128,128]{1,0:T(8,128)S(1)} %cholesky.118), custom_call_target="Cholesky" | custom-call | tf_op jit(solution)/shard_map/jit(cholesky)/cholesky | solution.py:24
  302.9 9.8 %custom-call.14 = f32[1,128,128]{1,2,0:T(8,128)S(1)} custom-call(f32[1,128,128]{2,1,0:T(8,128)S(1)} %get-tuple-element.27), custom_call_target="InvertDiagBlocksLowerTriangular" | custom-call | tf_op jit(solution)/shard_map/jit(cholesky)/cholesky | solution.py:24
  312.7 0.2 constant_dynamic-update-slice_fusion
  313.0 0.3 convolution_subtract_fusion.1
  313.2 11.7 %cholesky.105 = f32[128,128]{1,0:T(8,128)S(1)} custom-call(f32[128,128]{1,0:T(8,128)S(1)} %convolution_subtract_fusion.1), custom_call_target="Cholesky" | custom-call | tf_op jit(solution)/shard_map/jit(cholesky)/cholesky | solution.py:24
  325.0 0.6 compare_reduce_fusion
  327.0 0.1 triangular_solve.44
  327.0 4.1 while.1
  327.2 0.6 fusion.27
  327.8 1.4 bitcast_dynamic-update-slice_fusion.2
  329.2 0.6 fusion.27
  329.8 1.4 bitcast_dynamic-update-slice_fusion.2
  331.2 19.7 %custom-call.15 = f32[2,128,128]{1,2,0:T(8,128)S(1)} custom-call(f32[2,128,128]{2,1,0:T(8,128)S(1)} %get-tuple-element.9), custom_call_target="InvertDiagBlocksLowerTriangular" | custom-call | tf_op jit(solution)/shard_map/triangular_solve | solution.py:25
  350.9 0.6 fusion.15
  351.5 1.8 convolution_subtract_fusion
  353.3 1.1 convolution_convert_fusion.1
  354.4 2.3 fusion
  356.7 0.8 copy.6
  357.6 191.7 %all-reduce.9.cloned.1.call-done = f32[256,1024]{1,0:T(8,128)} async-done(((f32[256,1024]{1,0:T(8,128)}), f32[256,1024]{1,0:T(8,128)}) %all-reduce.9.cloned.1.call-update) | async-done | bytes 1048592 | tf_op jit(solution)/shard_map/psum | solution.py:30
  549.3 1.4 dynamic-slice_multiply_fusion
  (16 shorter events, 0.2 us)
Async XLA Ops:
  7.2 1.0 copy-start
  7.2 89.6 %all-reduce.5.cloned.1.call-start = ((), (), s32[]{:S(2)}) async-start(), calls=%async_computation | async-start | bytes 2097152 | tf_op jit(solution)/shard_map/psum | solution.py:21
  12.7 276.3 %all-reduce.7.cloned.1.call-start = ((), (), s32[]{:S(2)}) async-start(), calls=%async_computation.1 | async-start | bytes 524288 | tf_op jit(solution)/shard_map/psum | solution.py:23
  96.8 254.1 %copy-start.1 = (bf16[2048,256]{1,0:T(8,128)(2,1)S(1)}, bf16[2048,256]{1,0:T(8,128)(2,1)}, u32[]{:S(2)}) copy-start(bf16[2048,256]{1,0:T(8,128)(2,1)} %all-reduce.5.cloned.1.call-done) | copy-start | bytes 3145732
  99.6 449.7 %all-reduce.9.cloned.1.call-start = ((), (), s32[]{:S(2)}) async-start(), calls=%async_computation.2 | async-start | bytes 2097152 | tf_op jit(solution)/shard_map/psum | solution.py:30
  350.8 3.6 copy-start.2
Sparse Core Ops, SparseCore 0:
  12.8 83.8 all-reduce.4
  100.8 188.1 all-reduce.6
  356.9 192.3 all-reduce.8
where the time goes:
time: 558 us; the launch traced here: 557 us
  waiting for transfers between devices  465 us (83%)
  other arithmetic  57 us (10%)
  between operations  15.2 us (3%)
  matrix products  13.6 us (2%)
  local copies, waits for them, and re-layouts  6.02 us (1%)
    psum x1, waiting for transfers between devices, shards(): summed = lax.psum(full_proj, 'tok')  192 us
    psum x1, waiting for transfers between devices, shards(): gram_matrix = lax.psum(gram_matrix, 'tok') / all_tokens  189 us
    psum x1, waiting for transfers between devices, shards(): lax.psum(partial_value.astype(jnp.bfloat16), 'feat').astype(jnp.float32)  84 us
    another operation x6, other arithmetic, shards(): lower_factor = jnp.linalg.cholesky(gram_matrix)  33.9 us
    another operation x3, other arithmetic, shards(): lax.linalg.triangular_solve(lower_factor, sketch_rows.T, left_side=True,...  19.7 us
  transfers between devices with their start and end apart: 3, of which 3 were waited for; matrix products, arithmetic and copies ran while one was open for 0% of the time, Pallas kernels for 0%

commit v1 on v0

v1 whole, which is shorter than its diff:
```python
import math

import jax
import jax.numpy as jnp
from jax import lax
from jax.sharding import Mesh, PartitionSpec as P

TOK = ("y", "x", "core")
HIGHEST = lax.Precision.HIGHEST
F32 = jnp.float32
BF16 = jnp.bfloat16


def scatter(blocks, axes):
    return lax.all_to_all(blocks, axes, 0, 0)


def gather(block, axes):
    count = lax.axis_size(axes)
    return lax.all_to_all(jnp.broadcast_to(block[None], (count,) + block.shape), axes, 0, 0)


def factorize(gram):
    lower = jnp.linalg.cholesky(gram)
    eye = jnp.eye(gram.shape[0], dtype=F32)
    inverse = lax.linalg.triangular_solve(lower, eye, left_side=True, lower=True)
    return lower.T, inverse


def shards(activations, sketch):
    tokens, features = activations.shape
    cols = sketch.shape[1]
    all_tokens = tokens * lax.axis_size(TOK)
    n_feat = lax.axis_size("feat")
    chips = lax.axis_size(("y", "x"))
    n_y = lax.axis_size("y")
    near = lax.axis_size(("x", "core"))

    partial = jnp.dot(activations, sketch, preferred_element_type=F32).astype(BF16)
    parts = scatter(partial.reshape(n_feat, tokens // n_feat, cols), "feat")
    own = jnp.sum(parts.astype(F32), axis=0)
    rows = gather(own.astype(BF16), "feat").reshape(tokens, cols)

    gram = jnp.dot(own.T, own, precision=HIGHEST, preferred_element_type=F32)
    gram = jnp.sum(scatter(gram.reshape(chips, cols // chips, cols), ("y", "x")), axis=0)
    gram = jnp.sum(gather(gram, ("core", "feat")), axis=0)
    gram = gather(gram, ("y", "x")).reshape(cols, cols) / all_tokens

    cross = jnp.dot(rows.T, activations, preferred_element_type=F32)
    cross = cross.reshape(cols, near, features // near).transpose(1, 0, 2)
    cross = jnp.sum(scatter(cross, ("x", "core")), axis=0)

    factor, inverse = factorize(gram)
    proj = jnp.dot(inverse, cross, precision=HIGHEST, preferred_element_type=F32)
    own_rows = cols // lax.axis_size(TOK)
    proj = scatter(proj.reshape(-1, own_rows, features // near), TOK)
    proj = jnp.sum(proj.reshape(n_y, near, own_rows, features // near), axis=0)
    proj = proj.transpose(1, 0, 2).reshape(own_rows, features)
    return factor, proj / math.sqrt(all_tokens)


def solution(mesh):
    n_tok, n_feat = mesh.devices.shape
    fine = Mesh(mesh.devices.reshape(n_tok // 8, 4, 2, n_feat), TOK + ("feat",))
    in_specs = (P(TOK, "feat"), P("feat", None))
    out_specs = (P(), P(TOK, "feat"))
    return jax.shard_map(shards, mesh=fine, in_specs=in_specs, out_specs=out_specs, check_vma=False)
```

time: 558 us -> 191 us (0.34)
  waiting for transfers between devices: 465 us -> 14.3 us
  blocking collectives: 0 us -> 71.6 us
  starting transfers between devices: 0.12 us -> 20.5 us
  between operations: 15.2 us -> 2.19 us
  local copies, waits for them, and re-layouts: 6.02 us -> 16.7 us
    psum x3 -> x0, waiting for transfers between devices: 465 us -> none  [the longest x1 192 us: shards(): summed = lax.psum(full_proj, 'tok')]
    all_to_all x0 -> x3, blocking collectives: none -> 71.6 us  [the longest x2 57.8 us: scatter(): return lax.all_to_all(blocks, axes, 0, 0)]
    all_to_all x0 -> x4, starting transfers between devices: none -> 20.5 us  [the longest x2 12.1 us: scatter(): return lax.all_to_all(blocks, axes, 0, 0)]
    all_to_all x0 -> x4, waiting for transfers between devices: none -> 14.3 us  [the longest x2 10.3 us: scatter(): return lax.all_to_all(blocks, axes, 0, 0)]
    dot_general x0 -> x4, local copies, waits for them, and re-layouts: none -> 7.43 us  [the longest x1 6.5 us: shards(): cross = jnp.dot(rows.T, activations, preferred_element_type=F32)]
    another operation x9 -> x10, other arithmetic: 53.7 us -> 53.7 us  [the longest x6 33.9 us: factorize(): lower = jnp.linalg.cholesky(gram)]
  transfers between devices with their start and end apart: 3 -> 4, of which waited for: 3 -> 2; matrix products, arithmetic and copies ran while one was open for 0% -> 35% of each run, Pallas kernels for 0% -> 0%
where the time goes in v1:
time: 191 us; the launch traced here: 190 us
  blocking collectives  71.6 us (37%)
  other arithmetic  54.7 us (29%)
  starting transfers between devices  20.5 us (11%)
  local copies, waits for them, and re-layouts  16.7 us (9%)
  waiting for transfers between devices  14.3 us (7%)
  matrix products  9.95 us (5%)
  between operations  2.19 us (1%)
    all_to_all x2, blocking collectives, scatter(): return lax.all_to_all(blocks, axes, 0, 0)  57.8 us
    another operation x6, other arithmetic, factorize(): lower = jnp.linalg.cholesky(gram)  33.9 us
    another operation x4, other arithmetic, factorize(): lax.linalg.triangular_solve(lower, eye, left_side=True, lower=True)  19.7 us
    all_to_all x1, blocking collectives, gather(): lax.all_to_all(jnp.broadcast_to(block[None], (count,) + block.shape), axe...  13.7 us
    all_to_all x2, starting transfers between devices, scatter(): return lax.all_to_all(blocks, axes, 0, 0)  12.1 us
    all_to_all x2, waiting for transfers between devices, scatter(): return lax.all_to_all(blocks, axes, 0, 0)  10.3 us
    all_to_all x2, starting transfers between devices, gather(): lax.all_to_all(jnp.broadcast_to(block[None], (count,) + block.shape), axe...  8.45 us
    dot_general x1, local copies, waits for them, and re-layouts, shards(): cross = jnp.dot(rows.T, activations, preferred_element_type=F32)  6.5 us
  transfers between devices with their start and end apart: 4, of which 2 were waited for; matrix products, arithmetic and copies ran while one was open for 35% of the time, Pallas kernels for 0%

profile of v1, /device:TPU:1, one launch (start us, length us, event | category | flops | bytes accessed | tf_op | source)
XLA Modules:
  0.0 189.9 jit_solution(8874549124232062428)
XLA Ops:
  0.6 1.0 copy-done
  1.7 3.4 %convolution_convert_fusion = bf16[2048,256]{1,0:T(8,128)(2,1)S(1)} fusion(bf16[2048,1024]{1,0:T(8,128)(2,1)} %param.2, bf16[1024,256]{1,0:T(8,128)(2,1)S(1)} %copy-done), kind=kOutput, calls=%fused_computation.2 | convolution fusion | flops 1074266112 | bytes 5767168 | tf_op jit(solution)/shard_map/dot_general | solution.py:39
  5.1 37.9 %all_to_all.35 = bf16[8,256,256]{2,1,0:T(8,128)(2,1)S(1)} all-to-all(bf16[8,256,256]{2,1,0:T(8,128)(2,1)S(1)} %bitcast.66), channel_id=1, replica_groups=mesh['y'=8,'x'=4,'core'=2,'feat'=8] {'feat'}, dimensions={0} | all-to-all | bytes 2097152 | tf_op jit(solution)/shard_map/all_to_all | solution.py:15
  43.3 0.4 fusion.1
  43.7 19.9 %all_to_all.36 = f32[32,8,256]{2,1,0:T(8,128)S(1)} all-to-all(f32[32,8,256]{2,1,0:T(8,128)S(1)} %fusion.1), channel_id=1, replica_groups=mesh['y'=8,'x'=4,'core'=2,'feat'=8] {'y','x'}, dimensions={0} | all-to-all | bytes 524288 | tf_op jit(solution)/shard_map/all_to_all | solution.py:15
  63.7 13.7 %all_to_all.37 = f32[16,8,256]{2,1,0:T(8,128)S(1)} all-to-all(f32[16,8,256]{2,1,0:T(8,128)S(1)} %broadcast_in_dim.7), channel_id=1, replica_groups=mesh['y'=8,'x'=4,'core'=2,'feat'=8] {'core','feat'}, dimensions={0} | all-to-all | bytes 262144 | tf_op jit(solution)/shard_map/all_to_all | solution.py:20
  77.4 0.7 broadcast_in_dim.8
  78.2 3.9 %all-to-all-start.3 = ((f32[32,8,256]{2,1,0:T(8,128)}), f32[32,8,256]{2,1,0:T(8,128)S(1)}, u32[]{:S(2)}, u32[]{:S(2)}) async-start(f32[32,8,256]{2,1,0:T(8,128)} %broadcast_in_dim.8), calls=%async_computation.3 | async-start | bytes 524288 | tf_op jit(solution)/shard_map/all_to_all | solution.py:20
  82.1 6.5 %copy.35 = bf16[1024,2048]{1,0:T(8,128)(2,1)} copy(bf16[1024,2048]{0,1:T(8,128)(2,1)} %bitcast.64) | data formatting | bytes 8388608 | tf_op jit(solution)/shard_map/dot_general | solution.py:49
  88.7 4.0 %all-to-all-done.3 = f32[32,8,256]{2,1,0:T(8,128)S(1)} async-done(((f32[32,8,256]{2,1,0:T(8,128)}), f32[32,8,256]{2,1,0:T(8,128)S(1)}, u32[]{:S(2)}, u32[]{:S(2)}) %all-to-all-start.3) | async-done | bytes 262176 | tf_op jit(solution)/shard_map/all_to_all | solution.py:20
  92.7 1.0 broadcast_in_dim.9
  93.7 4.6 %all-to-all-start.4 = ((bf16[8,256,256]{1,2,0:T(8,128)(2,1)}), bf16[8,256,256]{1,2,0:T(8,128)(2,1)S(1)}, u32[]{:S(2)}, u32[]{:S(2)}) async-start(bf16[8,256,256]{1,2,0:T(8,128)(2,1)} %broadcast_in_dim.9), calls=%async_computation.4 | async-start | bytes 2097152 | tf_op jit(solution)/shard_map/all_to_all | solution.py:20
  98.5 11.7 %cholesky.50 = f32[128,128]{1,0:T(8,128)S(1)} custom-call(f32[128,128]{1,0:T(8,128)S(1)} %cholesky.118), custom_call_target="Cholesky" | custom-call | tf_op jit(solution)/shard_map/jit(cholesky)/cholesky | solution.py:24
  110.3 9.8 %custom-call.14 = f32[1,128,128]{1,2,0:T(8,128)S(1)} custom-call(f32[1,128,128]{2,1,0:T(8,128)S(1)} %get-tuple-element.35), custom_call_target="InvertDiagBlocksLowerTriangular" | custom-call | tf_op jit(solution)/shard_map/jit(cholesky)/cholesky | solution.py:24
  120.6 11.7 %cholesky.105 = f32[128,128]{1,0:T(8,128)S(1)} custom-call(f32[128,128]{1,0:T(8,128)S(1)} %convolution_subtract_fusion.1), custom_call_target="Cholesky" | custom-call | tf_op jit(solution)/shard_map/jit(cholesky)/cholesky | solution.py:24
  132.4 0.6 compare_reduce_fusion
  134.4 0.6 copy.30
  135.0 0.7 reshape.70
  135.7 4.4 %convolution_bitcast_fusion = f32[8,256,128]{2,1,0:T(8,128)} fusion(bf16[2048,256,1]{0,1,2:T(8,128)(2,1)S(1)} %reshape.70, bf16[8,128,2048]{2,1,0:T(8,128)(2,1)} %bitcast.65), kind=kOutput, calls=%fused_computation.4 | convolution fusion | flops 1073741824 | bytes 6291456 | tf_op jit(solution)/shard_map/dot_general | solution.py:49
  140.2 6.1 %all-to-all-start.5 = ((f32[8,256,128]{2,1,0:T(8,128)}), f32[8,256,128]{2,1,0:T(8,128)S(1)}, u32[]{:S(2)}, u32[]{:S(2)}) async-start(f32[8,256,128]{2,1,0:T(8,128)} %convolution_bitcast_fusion), calls=%async_computation.5 | async-start | bytes 2097152 | tf_op jit(solution)/shard_map/all_to_all | solution.py:15
  146.3 4.0 %while.1 = (s32[]{:T(128)}, f32[256,256]{1,0:T(8,128)S(1)}, s32[2,2]{1,0:T(2,128)S(1)}, f32[2,128,128]{2,1,0:T(8,128)S(1)}, s32[]{:T(128)}) while((s32[]{:T(128)}, f32[256,256]{1,0:T(8,128)S(1)}, s32[2,2]{1,0:T(2,128)S(1)}, f32[2,128,128]{2,1,0:T(8,128)S(1)}, s32[]{:T(128)}) %tuple.33), condition=%wide.while_cond, body=%wide.while_body.sunk | while | flops 2 | bytes 131189 | solution.py:26
  146.3 0.6 fusion.26
  146.9 1.4 bitcast_dynamic-update-slice_fusion.2
  148.3 0.6 fusion.26
  148.9 1.4 bitcast_dynamic-update-slice_fusion.2
  150.3 19.7 %custom-call.15 = f32[2,128,128]{1,2,0:T(8,128)S(1)} custom-call(f32[2,128,128]{2,1,0:T(8,128)S(1)} %get-tuple-element.9), custom_call_target="InvertDiagBlocksLowerTriangular" | custom-call | tf_op jit(solution)/shard_map/triangular_solve | solution.py:26
  171.0 0.4 fusion.4
  171.4 0.7 copy.33
  172.2 6.0 %all-to-all-start.6 = ((f32[64,4,128]{2,1,0:T(4,128)}), f32[64,4,128]{2,1,0:T(4,128)S(1)}, u32[]{:S(2)}, u32[]{:S(2)}) async-start(f32[64,4,128]{2,1,0:T(4,128)} %copy.33), calls=%async_computation.6 | async-start | bytes 262144 | tf_op jit(solution)/shard_map/all_to_all | solution.py:15
  178.2 0.8 copy.34
  179.0 10.3 %all-to-all-done.6 = f32[64,4,128]{2,1,0:T(4,128)S(1)} async-done(((f32[64,4,128]{2,1,0:T(4,128)}), f32[64,4,128]{2,1,0:T(4,128)S(1)}, u32[]{:S(2)}, u32[]{:S(2)}) %all-to-all-start.6) | async-done | bytes 131104 | tf_op jit(solution)/shard_map/all_to_all | solution.py:15
  189.3 0.6 multiply_bitcast_fusion.1
  (33 shorter events, 2.4 us)
Async XLA Ops:
  0.6 1.0 copy-start
  78.2 14.5 %all-to-all-start.3 = ((f32[32,8,256]{2,1,0:T(8,128)}), f32[32,8,256]{2,1,0:T(8,128)S(1)}, u32[]{:S(2)}, u32[]{:S(2)}) async-start(f32[32,8,256]{2,1,0:T(8,128)} %broadcast_in_dim.8), calls=%async_computation.3 | async-start | bytes 524288 | tf_op jit(solution)/shard_map/all_to_all | solution.py:20
  93.7 40.7 %all-to-all-start.4 = ((bf16[8,256,256]{1,2,0:T(8,128)(2,1)}), bf16[8,256,256]{1,2,0:T(8,128)(2,1)S(1)}, u32[]{:S(2)}, u32[]{:S(2)}) async-start(bf16[8,256,256]{1,2,0:T(8,128)(2,1)} %broadcast_in_dim.9), calls=%async_computation.4 | async-start | bytes 2097152 | tf_op jit(solution)/shard_map/all_to_all | solution.py:20
  140.2 30.8 %all-to-all-start.5 = ((f32[8,256,128]{2,1,0:T(8,128)}), f32[8,256,128]{2,1,0:T(8,128)S(1)}, u32[]{:S(2)}, u32[]{:S(2)}) async-start(f32[8,256,128]{2,1,0:T(8,128)} %convolution_bitcast_fusion), calls=%async_computation.5 | async-start | bytes 2097152 | tf_op jit(solution)/shard_map/all_to_all | solution.py:15
  172.2 17.1 %all-to-all-start.6 = ((f32[64,4,128]{2,1,0:T(4,128)}), f32[64,4,128]{2,1,0:T(4,128)S(1)}, u32[]{:S(2)}, u32[]{:S(2)}) async-start(f32[64,4,128]{2,1,0:T(4,128)} %copy.33), calls=%async_computation.6 | async-start | bytes 262144 | tf_op jit(solution)/shard_map/all_to_all | solution.py:15
